TPU v7x, 32 devices: a whole 2x2x4 slice. The times are simulated.
32 devices in a mesh: grp: 4 (over y, core), seq: 8 (over z, x).
Axes of the slice: x: 2, y: 2, z: 4, core: 2. Of those that a mesh axis runs over, the one named last changes fastest.
Arguments:
- queries: bfloat16 [4096, 2048], P(('grp', 'seq')), may hold values from -4.5 to 4.5
- keys: bfloat16 [4096, 2048], P(('grp', 'seq')), may hold values from -4.5 to 4.5
- values: bfloat16 [4096, 2048], P(('grp', 'seq')), may hold values from -6 to 6
Outputs:
- attended: bfloat16 [4096, 2048], P(('grp', 'seq'))
All inputs are finite; a program needn't handle non-finite values.
Results may differ from a plain program's by a relative error of at most 0.0034.
Values may be sent and summed in bfloat16 or wider, within the bound.
A program may use at most 64 MiB of HBM per device.

v0:
```python
import math

import jax
import jax.numpy as jnp
from jax import lax
from jax.sharding import PartitionSpec as P

HEADS = 16
BLOCK = 128
MID_ROWS = 16
FAR_ROWS = 512


def padded(cells, sides, width):
    for axis, dim in sides:
        count = lax.axis_size(axis)
        ends = count - 1
        head = lax.slice_in_dim(cells, 0, width, axis=dim)
        tail = lax.slice_in_dim(cells, cells.shape[dim] - width, cells.shape[dim], axis=dim)
        cells = jnp.concatenate(
            [
                lax.ppermute(tail, axis, [(i, (i + 1) % count) for i in range(ends)]),
                cells,
                lax.ppermute(head, axis, [((i + 1) % count, i) for i in range(ends)]),
            ],
            axis=dim,
        )
    return cells


def run_mean(array, run):
    lead = array.shape[:-2]
    rows = array.shape[-2]
    width = array.shape[-1]
    return jnp.mean(array.astype(jnp.float32).reshape(lead + (rows // run, run, width)), axis=-2)


def merge_levels(
    query_rows, mid_query, extended, group_pair, far_pair, first, last, seat, far_allowed
):
    rows, width = query_rows.shape
    head_dim = width // HEADS
    blocks = rows // BLOCK
    scale = 1.0 / math.sqrt(head_dim)
    tiled = extended.reshape(2, blocks + 2, BLOCK, HEADS, head_dim)
    window = jnp.concatenate([tiled[:, :-2], tiled[:, 1:-1], tiled[:, 2:]], axis=2)
    query_blocks = query_rows.reshape(blocks, BLOCK, HEADS, head_dim)
    near = (
        jnp.einsum("nqhd,nkhd->nhqk", query_blocks, window[0], preferred_element_type=jnp.float32)
        * scale
    )
    position = jnp.arange(3 * BLOCK)
    slot = jnp.arange(blocks)
    drop_left = first & (slot[:, None] == 0) & (position[None, :] < BLOCK)
    drop_right = last & (slot[:, None] == blocks - 1) & (position[None, :] >= 2 * BLOCK)
    near = jnp.where((drop_left | drop_right)[:, None, None, :], -jnp.inf, near)
    mid_local = mid_query.shape[0]
    count = group_pair.shape[1]
    ratio = BLOCK // MID_ROWS
    query_index = seat * mid_local + jnp.arange(mid_local)
    mid_allowed = jnp.abs(jnp.arange(count)[None, :] // ratio - query_index[:, None] // ratio) > 1
    query_heads = mid_query.reshape(mid_local, HEADS, head_dim)
    group_keys = group_pair[0].astype(jnp.float32).reshape(count, HEADS, head_dim)
    middle = (
        jnp.einsum("ahd,chd->ahc", query_heads, group_keys, precision=lax.Precision.HIGHEST) * scale
    )
    middle = jnp.where(mid_allowed[:, None, :], middle, -jnp.inf)
    far_count = far_pair.shape[1]
    far_keys = far_pair[0].astype(jnp.float32).reshape(far_count, HEADS, head_dim)
    distant = (
        jnp.einsum("ahd,chd->ahc", query_heads, far_keys, precision=lax.Precision.HIGHEST) * scale
    )
    distant = jnp.where(far_allowed[None, None, :], distant, -jnp.inf)
    near_top = jnp.max(near, axis=-1).transpose(0, 2, 1).reshape(rows, HEADS)
    mid_top = jnp.repeat(jnp.max(middle, axis=-1), MID_ROWS, axis=0)
    far_top = jnp.repeat(jnp.max(distant, axis=-1), MID_ROWS, axis=0)
    top = jnp.maximum(near_top, jnp.maximum(mid_top, far_top))
    near_weight = jnp.exp(near - top.reshape(blocks, BLOCK, HEADS).transpose(0, 2, 1)[..., None])
    near_total = jnp.sum(near_weight, axis=-1).transpose(0, 2, 1).reshape(rows, HEADS)
    near_numer = jnp.einsum(
        "nhqk,nkhd->nqhd",
        near_weight.astype(jnp.bfloat16),
        window[1],
        preferred_element_type=jnp.float32,
    ).reshape(rows, HEADS, head_dim)
    top_grouped = top.reshape(mid_local, MID_ROWS, HEADS)[..., None]
    mid_weight = jnp.exp(middle[:, None] - top_grouped).reshape(rows, HEADS, count)
    mid_total = jnp.sum(mid_weight, axis=-1)
    group_values = group_pair[1].reshape(count, HEADS, head_dim)
    mid_numer = jnp.einsum(
        "rhc,chd->rhd",
        mid_weight.astype(jnp.bfloat16),
        group_values,
        preferred_element_type=jnp.float32,
    )
    far_weight = jnp.exp(distant[:, None] - top_grouped).reshape(rows, HEADS, far_count)
    far_total = jnp.sum(far_weight, axis=-1)
    far_values = far_pair[1].reshape(far_count, HEADS, head_dim)
    far_numer = jnp.einsum(
        "rhc,chd->rhd",
        far_weight.astype(jnp.bfloat16),
        far_values,
        preferred_element_type=jnp.float32,
    )
    result = (near_numer + mid_numer + far_numer) / (near_total + mid_total + far_total)[..., None]
    return result.reshape(rows, width).astype(jnp.bfloat16)


def per_device(queries, keys, values):
    place = lax.axis_index(("grp", "seq"))
    shards = lax.axis_size(("grp", "seq"))
    seat = lax.axis_index("seq")
    group = lax.axis_index("grp")
    paired = jnp.stack([keys, values], axis=0)
    extended = padded(paired, ((("grp", "seq"), 1),), BLOCK)
    mid_query = run_mean(queries, MID_ROWS)
    mid_pair = run_mean(paired, MID_ROWS).astype(jnp.bfloat16)
    group_pair = lax.all_gather(mid_pair, "seq", axis=1, tiled=True)
    far_local = run_mean(group_pair, FAR_ROWS // MID_ROWS).astype(jnp.bfloat16)
    local_far = far_local.shape[1]
    far_pair = lax.all_gather(far_local, "grp", axis=1, tiled=True)
    far_allowed = jnp.arange(far_pair.shape[1]) // local_far != group
    return merge_levels(
        queries,
        mid_query,
        extended,
        group_pair,
        far_pair,
        place == 0,
        place == shards - 1,
        seat,
        far_allowed,
    )


def solution(mesh):
    return jax.shard_map(
        per_device,
        mesh=mesh,
        in_specs=(P(("grp", "seq"), None), P(("grp", "seq"), None), P(("grp", "seq"), None)),
        out_specs=P(("grp", "seq"), None),
        check_vma=False,
    )
```

profile of v0, /device:TPU:0, one launch (start us, length us, event | category | flops | bytes accessed | tf_op | source)
XLA Modules:
  0.0 101.6 jit_solution(4294198290084697954)
XLA Ops:
  0.0 1.4 %pad_maximum_fusion.1 = bf16[2,128,2048]{2,1,0:T(8,128)(2,1)S(1)} fusion(bf16[1,128,2048]{2,1,0:T(8,128)(2,1)} %bitcast.132, bf16[1,128,2048]{2,1,0:T(8,128)(2,1)} %bitcast.135), kind=kLoop, calls=%fused_computation.29 | loop fusion | flops 524288 | bytes 2097152 | tf_op jit(solution)/shard_map/stack | solution.py:114
  1.4 5.9 %collective-permute-start = (bf16[2,128,2048]{2,1,0:T(8,128)(2,1)S(1)}, bf16[2,128,2048]{2,1,0:T(8,128)(2,1)}, u32[]{:S(2)}, u32[]{:S(2)}) collective-permute-start(bf16[2,128,2048]{2,1,0:T(8,128)(2,1)S(1)} %pad_maximum_fusion.1), channel_id=1, source_target_pairs={{0,1},{1,2},{2,3},{3,4},{4,5},{5,6},{6,7},{7,8},{8,9},{9,10},{10,1... | collective-permute-start | bytes 3145736 | tf_op jit(solution)/shard_map/ppermute | solution.py:22
  7.2 1.3 %collective-permute-start.1 = (bf16[2,128,2048]{2,1,0:T(8,128)(2,1)S(1)}, bf16[2,128,2048]{2,1,0:T(8,128)(2,1)}, u32[]{:S(2)}, u32[]{:S(2)}) collective-permute-start(bf16[2,128,2048]{2,1,0:T(8,128)(2,1)S(1)} %pad_maximum_fusion.1), channel_id=1, source_target_pairs={{1,0},{2,1},{3,2},{4,3},{5,4},{6,5},{7,6},{8,7},{9,8},{10,9},{11,1... | collective-permute-start | bytes 3145736 | tf_op jit(solution)/shard_map/ppermute | solution.py:24
  8.5 1.6 %convert_reduce_fusion = f32[2,8,2048]{2,1,0:T(8,128)S(1)} fusion(bf16[1,8,16,2048]{3,2,1,0:T(8,128)(2,1)} %bitcast.133, bf16[1,8,16,2048]{3,2,1,0:T(8,128)(2,1)} %bitcast.136), kind=kLoop, calls=%fused_computation.7 | loop fusion | flops 1540096 | bytes 1179648 | tf_op jit(solution)/shard_map/reduce_sum | solution.py:35
  10.1 0.0 copy-start
  10.1 0.0 copy-start.1
  10.2 71.5 %all_gather.6 = bf16[2,64,2048]{2,1,0:T(8,128)(2,1)S(1)} all-gather(bf16[2,8,2048]{2,1,0:T(8,128)(2,1)S(1)} %multiply_convert_fusion), channel_id=1, replica_groups=mesh['grp'=4,'seq'=8] {'seq'}, dimensions={1}, use_global_device_ids=true | all-gather | bytes 589824 | tf_op jit(solution)/shard_map/all_gather | solution.py:118
  81.7 0.1 convert_reduce_fusion.1
  81.9 5.2 %all_gather.7 = bf16[2,8,2048]{2,0,1:T(2,128)(2,1)S(1)} all-gather(bf16[2,2,2048]{2,0,1:T(2,128)(2,1)S(1)} %copy.68), channel_id=1, replica_groups=mesh['grp'=4,'seq'=8] {'grp'}, dimensions={1}, use_global_device_ids=true | all-gather | bytes 81920 | tf_op jit(solution)/shard_map/all_gather | solution.py:121
  87.2 0.9 slice_reduce_fusion
  88.0 0.0 copy-done.2
  88.0 0.2 convert_reduce_fusion.2
  88.2 0.1 abs_compare_fusion
  88.3 0.2 fusion.48
  88.5 0.6 fusion.47
  89.1 0.1 copy.70
  89.2 0.7 copy.86
  89.9 0.1 copy.87
  89.9 0.1 copy.95
  90.0 0.2 sub.97
  90.2 0.8 sub.98
  91.0 0.0 collective-permute-done
  91.0 0.0 collective-permute-done.1
  91.0 0.0 copy-done
  91.0 0.0 copy-done.1
  91.1 1.7 %pad_maximum_fusion = bf16[2,384,2048]{2,1,0:T(8,128)(2,1)S(1)} fusion(bf16[2,128,2048]{2,1,0:T(8,128)(2,1)} %collective-permute-done.1, bf16[1,128,2048]{2,1,0:T(8,128)(2,1)S(1)} %bitcast.134, bf16[1,128,2048]{2,1,0:T(8,128)(2,1)S(1)} %bitcast.137, bf16[2,128,2048]{2,1,0:T(8,128)(2,1)} %collective-permute-done), kind=kLoop, calls=%fused_computation | loop fusion | flops 12582912 | bytes 6291456 | tf_op jit(solution)/shard_map/concatenate | solution.py:20
  92.8 1.0 copy.93
  93.8 0.5 fusion.46
  94.4 0.3 copy_dynamic-update-slice_fusion.2
  94.6 0.3 copy_dynamic-update-slice_fusion.1
  95.0 0.3 copy_dynamic-update-slice_fusion
  95.3 0.0 copy-start.4
  95.3 0.6 bitcast_reduce_fusion
  96.0 0.1 copy-done.4
  96.0 0.7 fusion.1
  96.7 1.2 %fusion.10 = f32[128,16,128]{0,2,1:T(8,128)S(1)} fusion(f32[16,384,128]{2,1,0:T(8,128)S(1)} %get-tuple-element.17, f32[16,128]{1,0:T(8,128)S(1)} %maximum_bitcast_fusion, pred[384]{0:T(512)(128)(4,1)S(1)} %fusion.39, bf16[2,1,384,16,128]{4,2,3,1,0:T(8,128)(2,1)S(1)} %copy_dynamic-update-slice_fusion), kind=kOutput, calls=%fused_computation.16 | convolution fusion | flops 204472320 | bytes 5775872 | tf_op jit(solution)/shard_map/nhqk,nkhd->nqhd/dot_general | solution.py:80
  98.0 0.0 copy-start.3
  98.0 0.1 copy.88
  98.1 0.1 copy.82
  98.2 0.7 exponential_reduce_fusion
  98.9 0.1 copy.81
  98.9 0.2 exponential_reduce_fusion.1
  99.2 0.1 reduce_sum.68
  99.2 0.1 copy.76
  99.3 0.3 fusion.22
  99.7 0.5 fusion.15
  100.2 0.4 fusion.16
  100.6 1.0 copy.83
  (19 shorter events, 0.2 us)
Async XLA Ops:
  0.0 88.0 %copy-start.2 = (bf16[128,2048]{1,0:T(8,128)(2,1)S(1)}, bf16[128,2048]{1,0:T(8,128)(2,1)}, u32[]{:S(2)}) copy-start(bf16[128,2048]{1,0:T(8,128)(2,1)} %param.3) | copy-start | bytes 1572868
  1.4 89.7 %collective-permute-start = (bf16[2,128,2048]{2,1,0:T(8,128)(2,1)S(1)}, bf16[2,128,2048]{2,1,0:T(8,128)(2,1)}, u32[]{:S(2)}, u32[]{:S(2)}) collective-permute-start(bf16[2,128,2048]{2,1,0:T(8,128)(2,1)S(1)} %pad_maximum_fusion.1), channel_id=1, source_target_pairs={{0,1},{1,2},{2,3},{3,4},{4,5},{5,6},{6,7},{7,8},{8,9},{9,10},{10,1... | collective-permute-start | bytes 3145736 | tf_op jit(solution)/shard_map/ppermute | solution.py:22
  7.2 83.8 %collective-permute-start.1 = (bf16[2,128,2048]{2,1,0:T(8,128)(2,1)S(1)}, bf16[2,128,2048]{2,1,0:T(8,128)(2,1)}, u32[]{:S(2)}, u32[]{:S(2)}) collective-permute-start(bf16[2,128,2048]{2,1,0:T(8,128)(2,1)S(1)} %pad_maximum_fusion.1), channel_id=1, source_target_pairs={{1,0},{2,1},{3,2},{4,3},{5,4},{6,5},{7,6},{8,7},{9,8},{10,9},{11,1... | collective-permute-start | bytes 3145736 | tf_op jit(solution)/shard_map/ppermute | solution.py:24
  10.1 80.9 %copy-start = (bf16[128,2048]{1,0:T(8,128)(2,1)S(1)}, bf16[128,2048]{1,0:T(8,128)(2,1)}, u32[]{:S(2)}) copy-start(bf16[128,2048]{1,0:T(8,128)(2,1)} %param.5) | copy-start | bytes 1572868
  10.1 80.9 %copy-start.1 = (bf16[128,2048]{1,0:T(8,128)(2,1)S(1)}, bf16[128,2048]{1,0:T(8,128)(2,1)}, u32[]{:S(2)}) copy-start(bf16[128,2048]{1,0:T(8,128)(2,1)} %param.4) | copy-start | bytes 1572868
  95.3 0.7 copy-start.4
  98.0 2.2 %copy-start.3 = (f32[128,16,8]{0,2,1:T(8,128)S(1)}, f32[128,16,8]{0,2,1:T(8,128)}, u32[]{:S(2)}) copy-start(f32[128,16,8]{0,2,1:T(8,128)} %sub.98) | copy-start | bytes 196612
  98.0 2.2 %copy-start.5 = (bf16[8,2048]{1,0:T(8,128)(2,1)S(1)}, bf16[8,2048]{1,0:T(8,128)(2,1)}, u32[]{:S(2)}) copy-start(bf16[8,2048]{1,0:T(8,128)(2,1)} %get-tuple-element.5) | copy-start | bytes 98308
where the time goes:
time: 102 us
  blocking collectives  76.7 us (75%)
  starting transfers between devices  7.17 us (7%)
  other arithmetic  7.02 us (7%)
  local copies, waits for them, and re-layouts  6.88 us (7%)
  matrix products  3.53 us (3%)
    all_gather x1, blocking collectives, per_device(): group_pair = lax.all_gather(mid_pair, 'seq', axis=1, tiled=True)  71.5 us
    ppermute x1, starting transfers between devices, padded(): lax.ppermute(tail, axis, [(i, (i + 1) % count) for i in range(ends)])  5.89 us
    all_gather x1, blocking collectives, per_device(): far_pair = lax.all_gather(far_local, 'grp', axis=1, tiled=True)  5.25 us
  transfers between devices with their start and end apart: 2, of which 0 were waited for; matrix products, arithmetic and copies ran while one was open for 6% of the time, Pallas kernels for 0%

commit v1 on v0

v1 whole, which is shorter than its diff:
```python
import functools
import math

import jax
import jax.numpy as jnp
from jax import lax
from jax.experimental import pallas as pl
from jax.experimental.pallas import tpu as pltpu
from jax.sharding import PartitionSpec as P

HEADS = 16
BLOCK = 128
MID_ROWS = 16
FAR_ROWS = 512
CHUNKS = 4
MESH = pl.DeviceIdType.MESH
F32 = jnp.float32
BF16 = jnp.bfloat16


def dot(a, b):
    return lax.dot_general(a, b, (((1,), (0,)), ((), ())), preferred_element_type=F32)


def dot_t(a, b):
    return lax.dot_general(a, b, (((1,), (1,)), ((), ())), preferred_element_type=F32)


def kernel(
    groups,
    seats,
    q_ref,
    k_ref,
    v_ref,
    o_ref,
    kv,
    qs,
    outs,
    mids,
    fars,
    local_sem,
    x_send,
    x_recv,
    own_send,
    own_recv,
    relay_send,
    relay_recv,
    mid_send,
    mid_recv,
    far_send,
    far_recv,
    out_send,
    out_recv,
    out_local,
):
    width = q_ref.shape[1]
    half = width // 2
    head_dim = width // HEADS
    cw = half // CHUNKS
    pairs = seats // 2
    total = groups * seats
    mid_pair = 2 * BLOCK // MID_ROWS
    mid_block = BLOCK // MID_ROWS
    mid_count = pairs * mid_pair
    far_local = mid_count * MID_ROWS // FAR_ROWS
    far_pad = fars.shape[2] // 2
    far_count = groups * far_pad
    scale = 1.0 / math.sqrt(head_dim)

    g = lax.axis_index("grp")
    s = lax.axis_index("seq")
    par = s % 2
    pair = s // 2
    place = g * seats + s
    mate = (g, s + 1 - 2 * par)
    left_place = (place + total - 2) % total
    right_place = (place + 2) % total
    left = (left_place // seats, left_place % seats)
    right = (right_place // seats, right_place % seats)
    has_left = place >= 2
    has_right = place < total - 2
    even = par == 0
    odd = par == 1
    mid_peers = [(g, (s + 2 * d) % seats) for d in range(1, pairs)]
    far_peers = [((g + d) % groups, s) for d in range(1, groups)]

    barrier = pltpu.get_barrier_semaphore()

    def greet(device):
        pl.semaphore_signal(barrier, inc=1, device_id=device, device_id_type=MESH)

    cross_left = (pair == 0) & has_left
    cross_right = (pair == pairs - 1) & has_right
    for device in [mate] + mid_peers + far_peers:
        greet(device)
    pl.when(cross_left)(lambda: greet(left))
    pl.when(cross_right)(lambda: greet(right))

    mine = par * half
    theirs = half - mine

    def cols(base, c):
        return pl.ds(pl.multiple_of(base + c * cw, 128), cw)

    def at(c):
        return pl.ds(c * cw, cw)

    def local_copies(c):
        return [
            pltpu.make_async_copy(
                k_ref.at[:, cols(mine, c)], kv.at[0, 1 + par, :, at(c)], local_sem.at[0, c]
            ),
            pltpu.make_async_copy(
                v_ref.at[:, cols(mine, c)], kv.at[1, 1 + par, :, at(c)], local_sem.at[1, c]
            ),
            pltpu.make_async_copy(
                q_ref.at[:, cols(mine, c)], qs.at[par, :, at(c)], local_sem.at[2, c]
            ),
        ]

    def remote(src, dst, send, recv, device):
        return pltpu.make_async_remote_copy(
            src_ref=src,
            dst_ref=dst,
            send_sem=send,
            recv_sem=recv,
            device_id=device,
            device_id_type=MESH,
        )

    def x_copies(c):
        targets = [
            (k_ref, kv.at[0, 1 + par, :, at(c)]),
            (v_ref, kv.at[1, 1 + par, :, at(c)]),
            (q_ref, qs.at[par, :, at(c)]),
        ]
        return [
            remote(src.at[:, cols(theirs, c)], dst, x_send.at[i, c], x_recv.at[i, c], mate)
            for i, (src, dst) in enumerate(targets)
        ]

    own_slot = 3 * (1 - par)
    relay_slot = 3 * par

    def own_copies(c, device):
        return [
            remote(
                src.at[:, cols(mine, c)],
                kv.at[i, own_slot, :, at(c)],
                own_send.at[i, c],
                own_recv.at[i, c],
                device,
            )
            for i, src in enumerate((k_ref, v_ref))
        ]

    def relay_copy(c, device):
        return remote(
            kv.at[:, 2 - par, :, at(c)],
            kv.at[:, relay_slot, :, at(c)],
            relay_send.at[c],
            relay_recv.at[c],
            device,
        )

    def mid_copies(c):
        return [
            remote(mids.at[c, pair], mids.at[c, pair], mid_send.at[d, c], mid_recv.at[d, c], peer)
            for d, peer in enumerate(mid_peers)
        ]

    def far_copies(c):
        return [
            remote(fars.at[c, g], fars.at[c, g], far_send.at[d, c], far_recv.at[d, c], peer)
            for d, peer in enumerate(far_peers)
        ]

    def out_remote(c):
        return remote(
            outs.at[1 - par, :, at(c)],
            o_ref.at[:, cols(mine, c)],
            out_send.at[c],
            out_recv.at[c],
            mate,
        )

    def out_own(c):
        return pltpu.make_async_copy(
            outs.at[par, :, at(c)], o_ref.at[:, cols(mine, c)], out_local.at[c]
        )

    def each(cond, make, act):
        @pl.when(cond)
        def _():
            for copy in make():
                act(copy)

    for c in range(CHUNKS):
        for copy in local_copies(c):
            copy.start()

    @pl.when(jnp.logical_not(has_left))
    def _():
        kv[:, 0] = jnp.zeros((2, BLOCK, half), BF16)

    @pl.when(jnp.logical_not(has_right))
    def _():
        kv[:, 3] = jnp.zeros((2, BLOCK, half), BF16)

    crossing = cross_left.astype(jnp.int32) + cross_right.astype(jnp.int32)
    pl.semaphore_wait(barrier, 1 + len(mid_peers) + len(far_peers) + crossing)

    start = lambda copy: copy.start()
    for c in range(CHUNKS):
        for copy in x_copies(c):
            copy.start()
        each(even & has_left, lambda c=c: own_copies(c, left), start)
        each(odd & has_right, lambda c=c: own_copies(c, right), start)

    run = lax.broadcasted_iota(jnp.int32, (mid_pair, 2 * BLOCK), 1) // MID_ROWS
    row = lax.broadcasted_iota(jnp.int32, (mid_pair, 2 * BLOCK), 0)
    mid_mean = jnp.where(run == row, 1.0 / MID_ROWS, 0.0).astype(BF16)
    ratio = FAR_ROWS // MID_ROWS
    run = lax.broadcasted_iota(jnp.int32, (far_pad, mid_count), 1) // ratio
    row = lax.broadcasted_iota(jnp.int32, (far_pad, mid_count), 0)
    far_mean = jnp.where(run == row, 1.0 / ratio, 0.0).astype(BF16)

    shape = (mid_pair, 1, mid_count)
    query_block = 2 * pair + lax.broadcasted_iota(jnp.int32, shape, 0) // mid_block
    key_block = lax.broadcasted_iota(jnp.int32, shape, 2) // mid_block
    mid_ok = jnp.abs(key_block - query_block) > 1
    shape = (mid_pair, 1, far_count)
    far_index = lax.broadcasted_iota(jnp.int32, shape, 2)
    far_ok = (far_index // far_pad != g) & (far_index % far_pad < far_local)
    bias = jnp.concatenate(
        [jnp.where(mid_ok, 0.0, -jnp.inf), jnp.where(far_ok, 0.0, -jnp.inf)], axis=2
    )

    def arrive(c):
        for copy in local_copies(c)[:2]:
            copy.wait()
        for copy in x_copies(c)[:2]:
            copy.wait_recv()
        each(even & has_right, lambda: [relay_copy(c, right)], start)
        each(odd & has_left, lambda: [relay_copy(c, left)], start)
        for i in range(2):
            rows = kv[i, 1:3, :, at(c)].reshape(2 * BLOCK, cw)
            mids[c, pair, i * mid_pair : (i + 1) * mid_pair, :] = dot(mid_mean, rows).astype(BF16)
        for copy in mid_copies(c):
            copy.start()

    def summarise(c):
        for copy in mid_copies(c):
            copy.wait_recv()
        for i in range(2):
            rows = mids[c, :, i * mid_pair : (i + 1) * mid_pair, :].reshape(mid_count, cw)
            fars[c, g, i * far_pad : (i + 1) * far_pad, :] = dot(far_mean, rows).astype(BF16)
        for copy in far_copies(c):
            copy.start()

    def attend(c):
        local_copies(c)[2].wait()
        x_copies(c)[2].wait_recv()
        recv = lambda copy: copy.wait_recv()
        each(even & has_right, lambda: own_copies(c, left), recv)
        each(odd & has_left, lambda: own_copies(c, right), recv)
        each(even & has_left, lambda: [relay_copy(c, right)], recv)
        each(odd & has_right, lambda: [relay_copy(c, left)], recv)
        for copy in far_copies(c):
            copy.wait_recv()
        for h in range(cw // head_dim):
            near_cols = pl.ds(c * cw + h * head_dim, head_dim)
            here = pl.ds(h * head_dim, head_dim)
            side = []
            for i in range(2):
                mid = mids[c, :, i * mid_pair : (i + 1) * mid_pair, here]
                far = fars[c, :, i * far_pad : (i + 1) * far_pad, here]
                side.append(
                    jnp.concatenate(
                        [mid.reshape(mid_count, head_dim), far.reshape(far_count, head_dim)], axis=0
                    )
                )
            query = qs[:, :, near_cols].reshape(2 * BLOCK, head_dim)
            coarse = dot_t(query, side[0]).reshape(mid_pair, MID_ROWS, mid_count + far_count)
            coarse = jnp.sum(coarse, axis=1, keepdims=True) * (scale / MID_ROWS) + bias
            coarse = jnp.broadcast_to(coarse, (mid_pair, MID_ROWS, mid_count + far_count))
            coarse = coarse.reshape(2 * BLOCK, mid_count + far_count)
            for j in range(2):
                rows = slice(j * BLOCK, (j + 1) * BLOCK)
                keys = kv[0, j : j + 3, :, near_cols].reshape(3 * BLOCK, head_dim)
                vals = kv[1, j : j + 3, :, near_cols].reshape(3 * BLOCK, head_dim)
                near = dot_t(query[rows], keys) * scale
                if j == 0:
                    edge = jnp.where(has_left, near[:, :BLOCK], -jnp.inf)
                    near = jnp.concatenate([edge, near[:, BLOCK:]], axis=1)
                else:
                    edge = jnp.where(has_right, near[:, 2 * BLOCK :], -jnp.inf)
                    near = jnp.concatenate([near[:, : 2 * BLOCK], edge], axis=1)
                scores = jnp.concatenate([near, coarse[rows]], axis=1)
                weight = jnp.exp(scores - jnp.max(scores, axis=1, keepdims=True))
                norm = jnp.sum(weight, axis=1, keepdims=True)
                numer = dot(weight.astype(BF16), jnp.concatenate([vals, side[1]], axis=0))
                outs[j, :, near_cols] = (numer * (1.0 / norm)).astype(BF16)
        out_remote(c).start()
        out_own(c).start()

    for t in range(CHUNKS + 2):
        if t < CHUNKS:
            arrive(t)
        if 1 <= t <= CHUNKS:
            summarise(t - 1)
        if t >= 2:
            attend(t - 2)

    sent = lambda copy: copy.wait_send()
    for c in range(CHUNKS):
        for copy in x_copies(c) + mid_copies(c) + far_copies(c):
            copy.wait_send()
        each(even & has_left, lambda: own_copies(c, left), sent)
        each(odd & has_right, lambda: own_copies(c, right), sent)
        each(even & has_right, lambda: [relay_copy(c, right)], sent)
        each(odd & has_left, lambda: [relay_copy(c, left)], sent)
        out_own(c).wait()
        out_remote(c).wait_send()
        out_remote(c).wait_recv()


def per_device(groups, seats, queries, keys, values):
    rows, width = queries.shape
    half = width // 2
    cw = half // CHUNKS
    pairs = seats // 2
    mid_pair = 2 * BLOCK // MID_ROWS
    far_local = pairs * 2 * BLOCK // FAR_ROWS
    far_pad = -(-far_local // 16) * 16
    dma = pltpu.SemaphoreType.DMA
    peers = max(pairs - 1, 1)
    others = max(groups - 1, 1)
    return pl.pallas_call(
        functools.partial(kernel, groups, seats),
        out_shape=jax.ShapeDtypeStruct((rows, width), BF16),
        in_specs=[pl.BlockSpec(memory_space=pl.ANY)] * 3,
        out_specs=pl.BlockSpec(memory_space=pl.ANY),
        scratch_shapes=[
            pltpu.VMEM((2, 4, BLOCK, half), BF16),
            pltpu.VMEM((2, BLOCK, half), BF16),
            pltpu.VMEM((2, BLOCK, half), BF16),
            pltpu.VMEM((CHUNKS, pairs, 2 * mid_pair, cw), BF16),
            pltpu.VMEM((CHUNKS, groups, 2 * far_pad, cw), BF16),
            dma((3, CHUNKS)),
            dma((3, CHUNKS)),
            dma((3, CHUNKS)),
            dma((2, CHUNKS)),
            dma((2, CHUNKS)),
            dma((CHUNKS,)),
            dma((CHUNKS,)),
            dma((peers, CHUNKS)),
            dma((peers, CHUNKS)),
            dma((others, CHUNKS)),
            dma((others, CHUNKS)),
            dma((CHUNKS,)),
            dma((CHUNKS,)),
            dma((CHUNKS,)),
        ],
        compiler_params=pltpu.CompilerParams(collective_id=0, has_side_effects=True),
    )(queries, keys, values)


def solution(mesh):
    groups, seats = mesh.shape["grp"], mesh.shape["seq"]
    spec = P(("grp", "seq"), None)
    return jax.shard_map(
        functools.partial(per_device, groups, seats),
        mesh=mesh,
        in_specs=(spec, spec, spec),
        out_specs=spec,
        check_vma=False,
    )
```

time: 102 us -> 45.9 us (0.45)
  blocking collectives: 76.7 us -> 0 us
  Pallas kernels: 0 us -> 43.9 us
  starting transfers between devices: 7.17 us -> 0 us
  other arithmetic: 7.02 us -> 0 us
  local copies, waits for them, and re-layouts: 6.88 us -> 1.88 us
  matrix products: 3.53 us -> 0 us
    all_gather x2 -> x0, blocking collectives: 76.7 us -> none  [the longest x1 71.5 us: per_device(): group_pair = lax.all_gather(mid_pair, 'seq', axis=1, tiled=True)]
    pallas_call x0 -> x1, Pallas kernels: none -> 43.9 us  [per_device(): pl.pallas_call(functools.partial(kernel, groups, seats), out_shape=jax.Sh...]
    ppermute x2 -> x0, starting transfers between devices: 7.17 us -> none  [the longest x1 5.89 us: padded(): lax.ppermute(tail, axis, [(i, (i + 1) % count) for i in range(ends)])]
    dot_general x6 -> x0, matrix products: 3.53 us -> none  [the longest x1 1.24 us: merge_levels(): jnp.einsum('nhqk,nkhd->nqhd', near_weight.astype(jnp.bfloat16), window[1]...]
    reduce_sum x6 -> x0, other arithmetic: 3.45 us -> none  [the longest x3 1.88 us: run_mean(): jnp.mean(array.astype(jnp.float32).reshape(lead + (rows // run, run, widt...]
    concatenate x1 -> x0, other arithmetic: 1.71 us -> none  [padded(): jnp.concatenate([lax.ppermute(tail, axis, [(i, (i + 1) % count) for i in...]
    slice x2 -> x0, local copies, waits for them, and re-layouts: 1.4 us -> none  [the longest x1 0.86 us: merge_levels(): far_values = far_pair[1].reshape(far_count, HEADS, head_dim)]
    another operation x1 -> x0, other arithmetic: 1.35 us -> none  [per_device(): paired = jnp.stack([keys, values], axis=0)]
  transfers between devices with their start and end apart: 2 -> 0, of which waited for: 0 -> 0; matrix products, arithmetic and copies ran while one was open for 6% -> 0% of each run, Pallas kernels for 0% -> 0%
where the time goes in v1:
time: 45.9 us; the launch traced here: 45.8 us
  Pallas kernels  43.9 us (96%)
  local copies, waits for them, and re-layouts  1.88 us (4%)
    pallas_call x1, Pallas kernels, per_device(): pl.pallas_call(functools.partial(kernel, groups, seats), out_shape=jax.Sh...  43.9 us
    unnamed x1, local copies, waits for them, and re-layouts  1.88 us

profile of v1, /device:TPU:0, one launch (start us, length us, event | category | flops | bytes accessed | tf_op | source)
XLA Modules:
  0.0 45.8 jit_solution(10743419195218780762)
XLA Ops:
  0.0 43.9 %shard_map.37 = bf16[128,2048]{1,0:T(8,128)(2,1)} custom-call(bf16[128,2048]{1,0:T(8,128)(2,1)} %q_ref.1, bf16[128,2048]{1,0:T(8,128)(2,1)} %k_ref.1, bf16[128,2048]{1,0:T(8,128)(2,1)} %v_ref.1), custom_call_target="tpu_custom_call" | custom-call | tf_op jit(solution)/shard_map/pallas_call | solution.py:339
  43.9 1.9 %copy.5 = bf16[128,2048]{1,0:T(8,128)(2,1)} copy(bf16[128,2048]{1,0:T(8,128)(2,1)} %shard_map.37) | data formatting | bytes 1048576

commit v2 on v1

v2 whole, which is shorter than its diff:
```python
import functools
import math

import jax
import jax.numpy as jnp
from jax import lax
from jax.experimental import pallas as pl
from jax.experimental.pallas import tpu as pltpu
from jax.sharding import PartitionSpec as P

HEADS = 16
BLOCK = 128
MID_ROWS = 16
FAR_ROWS = 512
CHUNKS = 4
DEPTH = 2
MESH = pl.DeviceIdType.MESH
F32 = jnp.float32
BF16 = jnp.bfloat16


def dot(a, b):
    return lax.dot_general(a, b, (((1,), (0,)), ((), ())), preferred_element_type=F32)


def dot_t(a, b):
    return lax.dot_general(a, b, (((1,), (1,)), ((), ())), preferred_element_type=F32)


def kernel(
    groups,
    seats,
    q_ref,
    k_ref,
    v_ref,
    o_ref,
    kv,
    qs,
    outs,
    rest,
    rest_mid,
    mids,
    fars,
    side,
    local_sem,
    rest_send,
    rest_recv,
    x_send,
    x_recv,
    own_send,
    own_recv,
    relay_send,
    relay_recv,
    mid_send,
    mid_recv,
    far_send,
    far_recv,
    out_send,
    out_recv,
    out_local,
):
    width = q_ref.shape[1]
    half = width // 2
    head_dim = width // HEADS
    cw = half // CHUNKS
    pairs = seats // 2
    total = groups * seats
    mid_pair = 2 * BLOCK // MID_ROWS
    mid_block = BLOCK // MID_ROWS
    mid_count = pairs * mid_pair
    far_local = mid_count * MID_ROWS // FAR_ROWS
    far_pad = fars.shape[1] // 2
    side_count = side.shape[1]
    scale = 1.0 / math.sqrt(head_dim)

    g = lax.axis_index("grp")
    s = lax.axis_index("seq")
    par = s % 2
    pair = s // 2
    place = g * seats + s
    mate = (g, s + 1 - 2 * par)
    left_place = (place + total - 2) % total
    right_place = (place + 2) % total
    left = (left_place // seats, left_place % seats)
    right = (right_place // seats, right_place % seats)
    has_left = place >= 2
    has_right = place < total - 2
    even = par == 0
    odd = par == 1
    mid_peers = [(g, (s + 2 * d) % seats) for d in range(1, pairs)]
    far_peers = [((g + d) % groups, s) for d in range(1, groups)]

    barrier = pltpu.get_barrier_semaphore()

    def greet(device):
        pl.semaphore_signal(barrier, inc=1, device_id=device, device_id_type=MESH)

    cross_left = (pair == 0) & has_left
    cross_right = (pair == pairs - 1) & has_right
    for device in [mate] + mid_peers + far_peers:
        greet(device)
    pl.when(cross_left)(lambda: greet(left))
    pl.when(cross_right)(lambda: greet(right))

    mine = par * half
    theirs = half - mine

    def cols(base, c):
        return pl.ds(pl.multiple_of(base + c * cw, 128), cw)

    def cols_half(base):
        return pl.ds(pl.multiple_of(base, 128), half)

    def at(c):
        return pl.ds(c * cw, cw)

    local = []
    for i, (src, dst) in enumerate(
        [
            (k_ref.at[:, cols_half(mine)], kv.at[0, 1 + par]),
            (v_ref.at[:, cols_half(mine)], kv.at[1, 1 + par]),
            (k_ref.at[:, cols_half(theirs)], rest.at[0]),
            (v_ref.at[:, cols_half(theirs)], rest.at[1]),
            (q_ref.at[:, cols_half(mine)], qs.at[par]),
        ]
    ):
        local.append(pltpu.make_async_copy(src, dst, local_sem.at[i]))

    def remote(src, dst, send, recv, device):
        return pltpu.make_async_remote_copy(
            src_ref=src,
            dst_ref=dst,
            send_sem=send,
            recv_sem=recv,
            device_id=device,
            device_id_type=MESH,
        )

    def x_copies(c):
        targets = [
            (k_ref, kv.at[0, 1 + par, :, at(c)]),
            (v_ref, kv.at[1, 1 + par, :, at(c)]),
            (q_ref, qs.at[par, :, at(c)]),
        ]
        return [
            remote(src.at[:, cols(theirs, c)], dst, x_send.at[i, c], x_recv.at[i, c], mate)
            for i, (src, dst) in enumerate(targets)
        ]

    own_slot = 3 * (1 - par)
    relay_slot = 3 * par

    def own_copies(c, device):
        return [
            remote(
                src.at[:, cols(mine, c)],
                kv.at[i, own_slot, :, at(c)],
                own_send.at[i, c],
                own_recv.at[i, c],
                device,
            )
            for i, src in enumerate((k_ref, v_ref))
        ]

    def relay_copy(c, device):
        return remote(
            kv.at[:, 2 - par, :, at(c)],
            kv.at[:, relay_slot, :, at(c)],
            relay_send.at[c],
            relay_recv.at[c],
            device,
        )

    rest_copy = remote(rest_mid, mids.at[pair, par], rest_send, rest_recv, mate)
    mid_copies = [
        remote(mids.at[pair], mids.at[pair], mid_send.at[d], mid_recv.at[d], peer)
        for d, peer in enumerate(mid_peers)
    ]
    far_copies = [
        remote(fars.at[g], fars.at[g], far_send.at[d], far_recv.at[d], peer)
        for d, peer in enumerate(far_peers)
    ]

    def out_remote(c):
        return remote(
            outs.at[1 - par, :, at(c)],
            o_ref.at[:, cols(mine, c)],
            out_send.at[c],
            out_recv.at[c],
            mate,
        )

    def out_own(c):
        return pltpu.make_async_copy(
            outs.at[par, :, at(c)], o_ref.at[:, cols(mine, c)], out_local.at[c]
        )

    def each(cond, make, act):
        @pl.when(cond)
        def _():
            for copy in make():
                act(copy)

    for copy in local:
        copy.start()

    @pl.when(jnp.logical_not(has_left))
    def _():
        kv[:, 0] = jnp.zeros((2, BLOCK, half), BF16)

    @pl.when(jnp.logical_not(has_right))
    def _():
        kv[:, 3] = jnp.zeros((2, BLOCK, half), BF16)

    def table(rows, columns):
        shape = (rows, columns)
        return (
            lax.broadcasted_iota(jnp.int32, shape, 0),
            lax.broadcasted_iota(jnp.int32, shape, 1),
        )

    row, col = table(mid_pair, 2 * BLOCK)
    mid_mean = jnp.where(col // MID_ROWS == row, 1.0 / MID_ROWS, 0.0).astype(BF16)
    for copy in local[:4]:
        copy.wait()
    mids[pair, par] = dot(mid_mean, kv[:, 1 + par].reshape(2 * BLOCK, half)).astype(BF16)
    rest_mid[...] = dot(mid_mean, rest[...].reshape(2 * BLOCK, half)).astype(BF16)

    crossing = cross_left.astype(jnp.int32) + cross_right.astype(jnp.int32)
    pl.semaphore_wait(barrier, 1 + len(mid_peers) + len(far_peers) + crossing)

    start = lambda copy: copy.start()
    start = lambda copy: copy.start()

    def push_pair(c):
        for copy in x_copies(c)[:2]:
            copy.start()
        each(even & has_left, lambda: own_copies(c, left), start)
        each(odd & has_right, lambda: own_copies(c, right), start)

    queue = [functools.partial(push_pair, c) for c in range(CHUNKS)]
    batch = CHUNKS // DEPTH
    for b in range(DEPTH):
        queue.append(
            lambda b=b: [x_copies(c)[2].start() for c in range(b * batch, (b + 1) * batch)]
        )
    rest_copy.start()
    for push in queue[:DEPTH]:
        push()
    rest_copy.wait_recv()
    for copy in mid_copies:
        copy.start()

    mid_raw = pairs * 2 * mid_pair
    far_raw = groups * 2 * far_pad
    ratio = FAR_ROWS // MID_ROWS

    def mid_place(raw):
        return raw // (2 * mid_block) * mid_block + raw % mid_block, raw // mid_block % 2

    def far_place(raw):
        return raw // (2 * far_pad) * far_pad + raw % far_pad + mid_count, raw // far_pad % 2

    row, col = table(2 * far_pad, mid_raw)
    index, kind = mid_place(col)
    far_hit = (index // ratio == row % far_pad) & (kind == row // far_pad)
    far_mean = jnp.where(far_hit, 1.0 / ratio, 0.0).astype(BF16)

    def pick(kind, place, raw):
        row, col = table(side_count, raw)
        index, found = place(col)
        return jnp.where((index == row) & (found == kind), 1.0, 0.0).astype(BF16)

    shape = (mid_pair, 1, side_count)
    query_block = 2 * pair + lax.broadcasted_iota(jnp.int32, shape, 0) // mid_block
    index = lax.broadcasted_iota(jnp.int32, shape, 2)
    far_index = index - mid_count
    mid_ok = (index < mid_count) & (jnp.abs(index // mid_block - query_block) > 1)
    far_ok = (far_index >= 0) & (far_index < groups * far_pad)
    far_ok = far_ok & (far_index // far_pad != g) & (far_index % far_pad < far_local)
    bias = jnp.where(mid_ok | far_ok, 0.0, -jnp.inf)

    def arrive(c):
        for copy in x_copies(c)[:2]:
            copy.wait_recv()
        queue[c + DEPTH]()
        each(even & has_right, lambda: [relay_copy(c, right)], start)
        each(odd & has_left, lambda: [relay_copy(c, left)], start)

    def summarise():
        for copy in mid_copies:
            copy.wait_recv()
        fars[g] = dot(far_mean, mids[...].reshape(mid_raw, half)).astype(BF16)
        for copy in far_copies:
            copy.start()

    def collect():
        for copy in far_copies:
            copy.wait_recv()
        for i in range(2):
            picked = dot(pick(i, mid_place, mid_raw), mids[...].reshape(mid_raw, half))
            picked += dot(pick(i, far_place, far_raw), fars[...].reshape(far_raw, half))
            side[i] = picked.astype(BF16)

    def attend(c):
        x_copies(c)[2].wait_recv()
        recv = lambda copy: copy.wait_recv()
        each(even & has_right, lambda: own_copies(c, left), recv)
        each(odd & has_left, lambda: own_copies(c, right), recv)
        each(even & has_left, lambda: [relay_copy(c, right)], recv)
        each(odd & has_right, lambda: [relay_copy(c, left)], recv)
        for h in range(cw // head_dim):
            near_cols = pl.ds(c * cw + h * head_dim, head_dim)
            query = qs[:, :, near_cols].reshape(2 * BLOCK, head_dim)
            coarse = dot_t(query, side[0, :, near_cols]).reshape(mid_pair, MID_ROWS, side_count)
            coarse = jnp.sum(coarse, axis=1, keepdims=True) * (scale / MID_ROWS) + bias
            coarse = jnp.broadcast_to(coarse, (mid_pair, MID_ROWS, side_count))
            coarse = coarse.reshape(2 * BLOCK, side_count)
            for j in range(2):
                rows = slice(j * BLOCK, (j + 1) * BLOCK)
                keys = kv[0, j : j + 3, :, near_cols].reshape(3 * BLOCK, head_dim)
                vals = kv[1, j : j + 3, :, near_cols].reshape(3 * BLOCK, head_dim)
                values = jnp.concatenate([vals, side[1, :, near_cols]], axis=0)
                near = dot_t(query[rows], keys) * scale
                if j == 0:
                    edge = jnp.where(has_left, near[:, :BLOCK], -jnp.inf)
                    near = jnp.concatenate([edge, near[:, BLOCK:]], axis=1)
                else:
                    edge = jnp.where(has_right, near[:, 2 * BLOCK :], -jnp.inf)
                    near = jnp.concatenate([near[:, : 2 * BLOCK], edge], axis=1)
                scores = jnp.concatenate([near, coarse[rows]], axis=1)
                weight = jnp.exp(scores - jnp.max(scores, axis=1, keepdims=True))
                norm = jnp.sum(weight, axis=1, keepdims=True)
                numer = dot(weight.astype(BF16), values)
                outs[j, :, near_cols] = (numer * (1.0 / norm)).astype(BF16)
        out_remote(c).start()
        out_own(c).start()

    for c in range(CHUNKS):
        if c == CHUNKS // 2:
            summarise()
        if c == CHUNKS - 1:
            collect()
        arrive(c)
    local[4].wait()
    for c in range(CHUNKS):
        attend(c)

    sent = lambda copy: copy.wait_send()
    for copy in [rest_copy] + mid_copies + far_copies:
        copy.wait_send()
    for c in range(CHUNKS):
        for copy in x_copies(c):
            copy.wait_send()
        each(even & has_left, lambda: own_copies(c, left), sent)
        each(odd & has_right, lambda: own_copies(c, right), sent)
        each(even & has_right, lambda: [relay_copy(c, right)], sent)
        each(odd & has_left, lambda: [relay_copy(c, left)], sent)
        out_own(c).wait()
        out_remote(c).wait_send()
        out_remote(c).wait_recv()


def per_device(groups, seats, queries, keys, values):
    rows, width = queries.shape
    half = width // 2
    pairs = seats // 2
    mid_pair = 2 * BLOCK // MID_ROWS
    far_local = pairs * 2 * BLOCK // FAR_ROWS
    far_pad = -(-far_local // 8) * 8
    mid_count = pairs * mid_pair
    side_count = -(-(mid_count + groups * far_pad) // 128) * 128
    dma = pltpu.SemaphoreType.DMA
    peers = max(pairs - 1, 1)
    others = max(groups - 1, 1)
    return pl.pallas_call(
        functools.partial(kernel, groups, seats),
        out_shape=jax.ShapeDtypeStruct((rows, width), BF16),
        in_specs=[pl.BlockSpec(memory_space=pl.ANY)] * 3,
        out_specs=pl.BlockSpec(memory_space=pl.ANY),
        scratch_shapes=[
            pltpu.VMEM((2, 4, BLOCK, half), BF16),
            pltpu.VMEM((2, BLOCK, half), BF16),
            pltpu.VMEM((2, BLOCK, half), BF16),
            pltpu.VMEM((2, BLOCK, half), BF16),
            pltpu.VMEM((mid_pair, half), BF16),
            pltpu.VMEM((pairs, 2, mid_pair, half), BF16),
            pltpu.VMEM((groups, 2 * far_pad, half), BF16),
            pltpu.VMEM((2, side_count, half), BF16),
            dma((5,)),
            dma(()),
            dma(()),
            dma((3, CHUNKS)),
            dma((3, CHUNKS)),
            dma((2, CHUNKS)),
            dma((2, CHUNKS)),
            dma((CHUNKS,)),
            dma((CHUNKS,)),
            dma((peers,)),
            dma((peers,)),
            dma((others,)),
            dma((others,)),
            dma((CHUNKS,)),
            dma((CHUNKS,)),
            dma((CHUNKS,)),
        ],
        compiler_params=pltpu.CompilerParams(collective_id=0, has_side_effects=True),
    )(queries, keys, values)


def solution(mesh):
    groups, seats = mesh.shape["grp"], mesh.shape["seq"]
    spec = P(("grp", "seq"), None)
    return jax.shard_map(
        functools.partial(per_device, groups, seats),
        mesh=mesh,
        in_specs=(spec, spec, spec),
        out_specs=spec,
        check_vma=False,
    )
```

time: 45.9 us -> 42.2 us (0.919)
  Pallas kernels: 43.9 us -> 40.1 us
    pallas_call x1, Pallas kernels: 43.9 us -> 40.1 us  [per_device(): pl.pallas_call(functools.partial(kernel, groups, seats), out_shape=jax.Sh...]
where the time goes in v2:
time: 42.2 us; the launch traced here: 42 us
  Pallas kernels  40.1 us (95%)
  local copies, waits for them, and re-layouts  1.88 us (4%)
    pallas_call x1, Pallas kernels, per_device(): pl.pallas_call(functools.partial(kernel, groups, seats), out_shape=jax.Sh...  40.1 us
    unnamed x1, local copies, waits for them, and re-layouts  1.88 us

profile of v2, /device:TPU:0, one launch (start us, length us, event | category | flops | bytes accessed | tf_op | source)
XLA Modules:
  0.0 42.0 jit_solution(18434649809412067090)
XLA Ops:
  0.0 40.1 %shard_map.37 = bf16[128,2048]{1,0:T(8,128)(2,1)} custom-call(bf16[128,2048]{1,0:T(8,128)(2,1)} %q_ref.1, bf16[128,2048]{1,0:T(8,128)(2,1)} %k_ref.1, bf16[128,2048]{1,0:T(8,128)(2,1)} %v_ref.1), custom_call_target="tpu_custom_call" | custom-call | tf_op jit(solution)/shard_map/pallas_call | solution.py:376
  40.1 1.9 %copy.5 = bf16[128,2048]{1,0:T(8,128)(2,1)} copy(bf16[128,2048]{1,0:T(8,128)(2,1)} %shard_map.37) | data formatting | bytes 1048576

commit v3 on v2

--- a/solution.py
+++ b/solution.py
@@ -375,9 +375,9 @@
     others = max(groups - 1, 1)
     return pl.pallas_call(
         functools.partial(kernel, groups, seats),
-        out_shape=jax.ShapeDtypeStruct((rows, width), BF16),
+        out_shape=pltpu.VMEM((rows, width), BF16),
         in_specs=[pl.BlockSpec(memory_space=pl.ANY)] * 3,
-        out_specs=pl.BlockSpec(memory_space=pl.ANY),
+        out_specs=pl.BlockSpec(memory_space=pltpu.VMEM),
         scratch_shapes=[
             pltpu.VMEM((2, 4, BLOCK, half), BF16),
             pltpu.VMEM((2, BLOCK, half), BF16),

time: 42.2 us -> 40.9 us (0.969)
  local copies, waits for them, and re-layouts: 1.88 us -> 0.8 us
    unnamed x1, local copies, waits for them, and re-layouts: 1.88 us -> 0.8 us
where the time goes in v3:
time: 40.9 us; the launch traced here: 40.8 us
  Pallas kernels  40 us (98%)
  local copies, waits for them, and re-layouts  0.8 us (2%)
    pallas_call x1, Pallas kernels, per_device(): pl.pallas_call(functools.partial(kernel, groups, seats), out_shape=pltpu....  40 us

profile of v3, /device:TPU:0, one launch (start us, length us, event | category | flops | bytes accessed | tf_op | source)
XLA Modules:
  0.0 40.8 jit_solution(4667406179157848383)
XLA Ops:
  0.0 40.0 %shard_map.37 = bf16[128,2048]{1,0:T(8,128)(2,1)S(1)} custom-call(bf16[128,2048]{1,0:T(8,128)(2,1)} %q_ref.1, bf16[128,2048]{1,0:T(8,128)(2,1)} %k_ref.1, bf16[128,2048]{1,0:T(8,128)(2,1)} %v_ref.1), custom_call_target="tpu_custom_call" | custom-call | tf_op jit(solution)/shard_map/pallas_call | solution.py:376
  40.0 0.8 %copy.5 = bf16[128,2048]{1,0:T(8,128)(2,1)} copy(bf16[128,2048]{1,0:T(8,128)(2,1)S(1)} %shard_map.37) | data formatting | bytes 1048576

commit v4 on v3

--- a/solution.py
+++ b/solution.py
@@ -14,6 +14,7 @@
 FAR_ROWS = 512
 CHUNKS = 4
 DEPTH = 2
+BENT = tuple(range(0, CHUNKS - 1, 2))
 MESH = pl.DeviceIdType.MESH
 F32 = jnp.float32
 BF16 = jnp.bfloat16
@@ -42,6 +43,10 @@
     mids,
     fars,
     side,
+    bent,
+    bent_send,
+    bent_recv,
+    pass_send,
     local_sem,
     rest_send,
     rest_recv,
@@ -90,13 +95,22 @@
     mid_peers = [(g, (s + 2 * d) % seats) for d in range(1, pairs)]
     far_peers = [((g + d) % groups, s) for d in range(1, groups)]
 
+    cross_left = (pair == 0) & has_left
+    cross_right = (pair == pairs - 1) & has_right
+    bend_left = cross_left & (g % 2 == 0)
+    bend_right = cross_right & (g % 2 == 1)
+    via_left = ((g + groups - 1) % groups, s)
+    via_right = ((g + 1) % groups, s)
+    pass_left = (pair == 0) & (g % 2 == 1) & (g < groups - 1)
+    pass_right = (pair == pairs - 1) & (g % 2 == 0) & (g > 0)
+    end_left = (g, (s + seats - 2) % seats)
+    end_right = (g, (s + 2) % seats)
+
     barrier = pltpu.get_barrier_semaphore()
 
     def greet(device):
         pl.semaphore_signal(barrier, inc=1, device_id=device, device_id_type=MESH)
 
-    cross_left = (pair == 0) & has_left
-    cross_right = (pair == pairs - 1) & has_right
     for device in [mate] + mid_peers + far_peers:
         greet(device)
     pl.when(cross_left)(lambda: greet(left))
@@ -171,6 +185,51 @@
             device,
         )
 
+    def bend_own(c, device):
+        return [
+            remote(
+                src.at[:, cols(mine, c)],
+                bent.at[i, :, at(c)],
+                bent_send.at[i, c],
+                bent_recv.at[i, c],
+                device,
+            )
+            for i, src in enumerate((k_ref, v_ref))
+        ]
+
+    def bend_relay(c, device):
+        return [
+            remote(
+                kv.at[i, 2 - par, :, at(c)],
+                bent.at[i, :, at(c)],
+                bent_send.at[i, c],
+                bent_recv.at[i, c],
+                device,
+            )
+            for i in range(2)
+        ]
+
+    def pass_own(c, device):
+        return [
+            remote(
+                bent.at[i, :, at(c)],
+                kv.at[i, own_slot, :, at(c)],
+                pass_send.at[i, c],
+                own_recv.at[i, c],
+                device,
+            )
+            for i in range(2)
+        ]
+
+    def pass_relay(c, device):
+        return remote(
+            bent.at[:, :, at(c)],
+            kv.at[:, relay_slot, :, at(c)],
+            pass_send.at[0, c],
+            relay_recv.at[c],
+            device,
+        )
+
     rest_copy = remote(rest_mid, mids.at[pair, par], rest_send, rest_recv, mate)
     mid_copies = [
         remote(mids.at[pair], mids.at[pair], mid_send.at[d], mid_recv.at[d], peer)
@@ -201,6 +260,32 @@
             for copy in make():
                 act(copy)
 
+    def own_each(c, act):
+        lefts, rights = even & has_left, odd & has_right
+        if c in BENT:
+            each(even & bend_left, lambda: bend_own(c, via_left), act)
+            each(odd & bend_right, lambda: bend_own(c, via_right), act)
+            lefts = lefts & jnp.logical_not(bend_left)
+            rights = rights & jnp.logical_not(bend_right)
+        each(lefts, lambda: own_copies(c, left), act)
+        each(rights, lambda: own_copies(c, right), act)
+
+    def relay_each(c, act):
+        lefts, rights = odd & has_left, even & has_right
+        if c in BENT:
+            each(odd & bend_left, lambda: bend_relay(c, via_left), act)
+            each(even & bend_right, lambda: bend_relay(c, via_right), act)
+            lefts = lefts & jnp.logical_not(bend_left)
+            rights = rights & jnp.logical_not(bend_right)
+        each(rights, lambda: [relay_copy(c, right)], act)
+        each(lefts, lambda: [relay_copy(c, left)], act)
+
+    def pass_each(c, act):
+        each(even & pass_left, lambda: pass_own(c, end_left), act)
+        each(odd & pass_right, lambda: pass_own(c, end_right), act)
+        each(odd & pass_left, lambda: [pass_relay(c, end_left)], act)
+        each(even & pass_right, lambda: [pass_relay(c, end_right)], act)
+
     for copy in local:
         copy.start()
 
@@ -235,8 +320,7 @@
     def push_pair(c):
         for copy in x_copies(c)[:2]:
             copy.start()
-        each(even & has_left, lambda: own_copies(c, left), start)
-        each(odd & has_right, lambda: own_copies(c, right), start)
+        own_each(c, start)
 
     queue = [functools.partial(push_pair, c) for c in range(CHUNKS)]
     batch = CHUNKS // DEPTH
@@ -280,12 +364,16 @@
     far_ok = far_ok & (far_index // far_pad != g) & (far_index % far_pad < far_local)
     bias = jnp.where(mid_ok | far_ok, 0.0, -jnp.inf)
 
+    landed = lambda copy: copy.wait_recv()
+
     def arrive(c):
         for copy in x_copies(c)[:2]:
             copy.wait_recv()
         queue[c + DEPTH]()
-        each(even & has_right, lambda: [relay_copy(c, right)], start)
-        each(odd & has_left, lambda: [relay_copy(c, left)], start)
+        relay_each(c, start)
+        if c - 1 in BENT:
+            each(pass_left | pass_right, lambda: bend_own(c - 1, via_left), landed)
+            pass_each(c - 1, start)
 
     def summarise():
         for copy in mid_copies:
@@ -352,10 +440,10 @@
     for c in range(CHUNKS):
         for copy in x_copies(c):
             copy.wait_send()
-        each(even & has_left, lambda: own_copies(c, left), sent)
-        each(odd & has_right, lambda: own_copies(c, right), sent)
-        each(even & has_right, lambda: [relay_copy(c, right)], sent)
-        each(odd & has_left, lambda: [relay_copy(c, left)], sent)
+        own_each(c, sent)
+        relay_each(c, sent)
+        if c in BENT:
+            pass_each(c, sent)
         out_own(c).wait()
         out_remote(c).wait_send()
         out_remote(c).wait_recv()
@@ -387,6 +475,10 @@
             pltpu.VMEM((pairs, 2, mid_pair, half), BF16),
             pltpu.VMEM((groups, 2 * far_pad, half), BF16),
             pltpu.VMEM((2, side_count, half), BF16),
+            pltpu.VMEM((2, BLOCK, half), BF16),
+            dma((2, CHUNKS)),
+            dma((2, CHUNKS)),
+            dma((2, CHUNKS)),
             dma((5,)),
             dma(()),
             dma(()),

time: 40.9 us -> 39.1 us (0.956)
  the two profiles are of different devices: /device:TPU:0 before, /device:TPU:4 now
where the time goes in v4:
time: 39.1 us; the launch traced here: 39 us
  Pallas kernels  38.2 us (98%)
  local copies, waits for them, and re-layouts  0.8 us (2%)
    pallas_call x1, Pallas kernels, per_device(): pl.pallas_call(functools.partial(kernel, groups, seats), out_shape=pltpu....  38.2 us
    unnamed x1, local copies, waits for them, and re-layouts  0.8 us

profile of v4, /device:TPU:4, one launch (start us, length us, event | category | flops | bytes accessed | tf_op | source)
XLA Modules:
  0.0 39.0 jit_solution(1331538592524914755)
XLA Ops:
  0.0 38.2 %shard_map.37 = bf16[128,2048]{1,0:T(8,128)(2,1)S(1)} custom-call(bf16[128,2048]{1,0:T(8,128)(2,1)} %q_ref.1, bf16[128,2048]{1,0:T(8,128)(2,1)} %k_ref.1, bf16[128,2048]{1,0:T(8,128)(2,1)} %v_ref.1), custom_call_target="tpu_custom_call" | custom-call | tf_op jit(solution)/shard_map/pallas_call | solution.py:464
  38.2 0.8 %copy.5 = bf16[128,2048]{1,0:T(8,128)(2,1)} copy(bf16[128,2048]{1,0:T(8,128)(2,1)S(1)} %shard_map.37) | data formatting | bytes 1048576

commit v5 on v4

--- a/solution.py
+++ b/solution.py
@@ -12,7 +12,7 @@
 BLOCK = 128
 MID_ROWS = 16
 FAR_ROWS = 512
-CHUNKS = 4
+CHUNKS = 8
 DEPTH = 2
 BENT = tuple(range(0, CHUNKS - 1, 2))
 MESH = pl.DeviceIdType.MESH

time: 39.1 us -> 38.4 us (0.982)
  the two profiles are of different devices: /device:TPU:4 before, /device:TPU:0 now
where the time goes in v5:
time: 38.4 us; the launch traced here: 38 us
  Pallas kernels  37.2 us (97%)
  local copies, waits for them, and re-layouts  0.8 us (2%)
    pallas_call x1, Pallas kernels, per_device(): pl.pallas_call(functools.partial(kernel, groups, seats), out_shape=pltpu....  37.2 us
    unnamed x1, local copies, waits for them, and re-layouts  0.8 us

profile of v5, /device:TPU:0, one launch (start us, length us, event | category | flops | bytes accessed | tf_op | source)
XLA Modules:
  0.0 38.0 jit_solution(2915148959697874604)
XLA Ops:
  0.0 37.2 %shard_map.37 = bf16[128,2048]{1,0:T(8,128)(2,1)S(1)} custom-call(bf16[128,2048]{1,0:T(8,128)(2,1)} %q_ref.1, bf16[128,2048]{1,0:T(8,128)(2,1)} %k_ref.1, bf16[128,2048]{1,0:T(8,128)(2,1)} %v_ref.1), custom_call_target="tpu_custom_call" | custom-call | tf_op jit(solution)/shard_map/pallas_call | solution.py:464
  37.2 0.8 %copy.5 = bf16[128,2048]{1,0:T(8,128)(2,1)} copy(bf16[128,2048]{1,0:T(8,128)(2,1)S(1)} %shard_map.37) | data formatting | bytes 1048576

commit v6 on v5

--- a/solution.py
+++ b/solution.py
@@ -318,9 +318,9 @@
     start = lambda copy: copy.start()
 
     def push_pair(c):
+        own_each(c, start)
         for copy in x_copies(c)[:2]:
             copy.start()
-        own_each(c, start)
 
     queue = [functools.partial(push_pair, c) for c in range(CHUNKS)]
     batch = CHUNKS // DEPTH
@@ -369,8 +369,8 @@
     def arrive(c):
         for copy in x_copies(c)[:2]:
             copy.wait_recv()
+        relay_each(c, start)
         queue[c + DEPTH]()
-        relay_each(c, start)
         if c - 1 in BENT:
             each(pass_left | pass_right, lambda: bend_own(c - 1, via_left), landed)
             pass_each(c - 1, start)

time: 38.4 us -> 38.4 us (level)
  no operation moved by 1% of the time
where the time goes in v6:
time: 38.4 us; the launch traced here: 38 us
  Pallas kernels  37.2 us (97%)
  local copies, waits for them, and re-layouts  0.8 us (2%)
    pallas_call x1, Pallas kernels, per_device(): pl.pallas_call(functools.partial(kernel, groups, seats), out_shape=pltpu....  37.2 us
    unnamed x1, local copies, waits for them, and re-layouts  0.8 us

profile of v6, /device:TPU:0, one launch (start us, length us, event | category | flops | bytes accessed | tf_op | source)
XLA Modules:
  0.0 38.0 jit_solution(18237787181313121416)
XLA Ops:
  0.0 37.2 %shard_map.37 = bf16[128,2048]{1,0:T(8,128)(2,1)S(1)} custom-call(bf16[128,2048]{1,0:T(8,128)(2,1)} %q_ref.1, bf16[128,2048]{1,0:T(8,128)(2,1)} %k_ref.1, bf16[128,2048]{1,0:T(8,128)(2,1)} %v_ref.1), custom_call_target="tpu_custom_call" | custom-call | tf_op jit(solution)/shard_map/pallas_call | solution.py:464
  37.2 0.8 %copy.5 = bf16[128,2048]{1,0:T(8,128)(2,1)} copy(bf16[128,2048]{1,0:T(8,128)(2,1)S(1)} %shard_map.37) | data formatting | bytes 1048576
